TPU v7x, 32 devices: a whole 2x2x4 slice. The times are simulated.
32 devices in a mesh: groups: 2 (over x), rows: 16 (over z, y, core).
Axes of the slice: x: 2, y: 2, z: 4, core: 2. Of those that a mesh axis runs over, the one named last changes fastest.
Arguments:
- image_query: bfloat16 [12288, 2048], P(('groups', 'rows')), parts along dimension 0, may hold values from -40 to 40
- image_pairs: bfloat16 [2, 12288, 2048], P(None, ('groups', 'rows')), parts along dimension 1, may hold values from -6 to 6
- text_query: bfloat16 [512, 2048], P(('groups', 'rows')), parts along dimension 0, may hold values from -40 to 40
- text_pairs: bfloat16 [2, 512, 2048], P(None, ('groups', 'rows')), parts along dimension 1, may hold values from -6 to 6
- text_mask: int32 [512], P('groups'), parts along dimension 0, may hold values 0 or 1
- window_offsets: int32 [16, 2], replicated, may hold values from -1 to 1, as said below
- timestep: int32 [1], replicated, may hold values from 0 to 49
- gate_table: float32 [50, 2, 2048], replicated, may hold values from 0.5 to 2
Outputs:
- image_out: bfloat16 [12288, 2048], P(('groups', 'rows')), parts along dimension 0
- text_out: bfloat16 [512, 2048], P(('groups', 'rows')), parts along dimension 0
There are 2 independent parts, one for each index of `groups`. A program takes and returns all parts, laid end to end along the dimension named above; an argument that names none is the same for every part. Nothing has to cross between parts.
Inputs may be any that keep to these rules, and one draw needn't show every extreme that they name: window_offsets[h, 0] is -1 or 0 and window_offsets[h, 1] is 0 or 1; some head has -1 and some head has 1.
All inputs are finite; a program needn't handle non-finite values.
Results may differ from a plain program's by a relative error of at most 0.02.
Values may be sent and summed in bfloat16 or wider, within the bound.
A program may use at most 128 MiB of HBM per device.

v0:
```python
import math
import jax
import jax.numpy as jnp
from jax import lax
from jax.sharding import PartitionSpec as P

TILE = 384
masked_score = -1e30


def extended_2(cells, sides, width):
    for axis, dim in sides:
        count = lax.axis_size(axis)
        ends = count - 1
        head = lax.slice_in_dim(cells, 0, width, axis=dim)
        tail = lax.slice_in_dim(cells, cells.shape[dim] - width, cells.shape[dim], axis=dim)
        cells = jnp.concatenate(
            [
                lax.ppermute(tail, axis, [(i, (i + 1) % count) for i in range(ends)]),
                cells,
                lax.ppermute(head, axis, [((i + 1) % count, i) for i in range(ends)]),
            ],
            axis=dim,
        )
    return cells


def attend_tiles(queries, key_rows, value_rows, allowed, scaling):
    scores = (
        jnp.einsum("tqhe,tkhe->tqhk", queries, key_rows, preferred_element_type=jnp.float32)
        * scaling
    )
    scores = jnp.where(allowed, scores, masked_score)
    maxima = jnp.max(scores, axis=-1)
    exponent = jnp.where(allowed, jnp.exp(scores - maxima[..., None]), 0.0)
    totals = jnp.sum(exponent, axis=-1)
    summed = jnp.einsum(
        "tqhk,tkhe->tqhe",
        exponent.astype(jnp.bfloat16),
        value_rows,
        preferred_element_type=jnp.float32,
    )
    return (maxima, totals, summed.astype(jnp.bfloat16))


def attend_rows(queries, key_rows, value_rows, allowed, scaling):
    scores = (
        jnp.einsum("qhe,khe->qhk", queries, key_rows, preferred_element_type=jnp.float32) * scaling
    )
    scores = jnp.where(allowed, scores, masked_score)
    maxima = jnp.max(scores, axis=-1)
    exponent = jnp.where(allowed, jnp.exp(scores - maxima[..., None]), 0.0)
    totals = jnp.sum(exponent, axis=-1)
    summed = jnp.einsum(
        "qhk,khe->qhe",
        exponent.astype(jnp.bfloat16),
        value_rows,
        preferred_element_type=jnp.float32,
    )
    return (maxima, totals, summed.astype(jnp.bfloat16))


def combine_groups(groups):
    largest = groups[0][0]
    for member in groups[1:]:
        largest = jnp.maximum(largest, member[0])
    totals = 0.0
    summed = 0.0
    for member in groups:
        factor = jnp.exp(member[0] - largest)
        totals = totals + member[1] * factor
        summed = summed + member[2].astype(jnp.float32) * factor[..., None]
    return summed / totals[..., None]


def on_device(
    image_query,
    image_pairs,
    text_query,
    text_pairs,
    text_mask,
    window_offsets,
    timestep,
    gate_table,
):
    rows_dev, width = image_query.shape
    tiles_dev = rows_dev // TILE
    head_count = window_offsets.shape[0]
    head_width = width // head_count
    scaling = 1.0 / math.sqrt(head_width)
    position = lax.axis_index("rows")
    tiles_all = tiles_dev * lax.axis_size("rows")
    first_tile = position * tiles_dev
    reach_back = window_offsets[:, 0]
    reach_ahead = window_offsets[:, 1]
    text_queries, text_gathered = (
        lax.all_gather(text_query, "rows", axis=0, tiled=True),
        lax.all_gather(text_pairs, "rows", axis=1, tiled=True),
    )
    text_keys = text_gathered[0].reshape(-1, head_count, head_width)
    text_values = text_gathered[1].reshape(-1, head_count, head_width)
    text_allowed = (text_mask == 1)[None, None, :]
    queries = image_query.reshape(tiles_dev, TILE, head_count, head_width)
    local_keys = image_pairs[0].reshape(tiles_dev, TILE, head_count, head_width)
    local_values = image_pairs[1].reshape(tiles_dev, TILE, head_count, head_width)

    def permitted(offset):
        target = first_tile + jnp.arange(tiles_dev, dtype=jnp.int32) + offset
        inside = (target >= 0) & (target < tiles_all)
        within = (reach_back <= offset) & (offset <= reach_ahead)
        return (inside[:, None] & within[None, :])[:, None, :, None]

    flat_queries = image_query.reshape(rows_dev, head_count, head_width)
    text_group = attend_rows(flat_queries, text_keys, text_values, text_allowed, scaling)
    text_group = (
        text_group[0].reshape(tiles_dev, TILE, head_count),
        text_group[1].reshape(tiles_dev, TILE, head_count),
        text_group[2].reshape(tiles_dev, TILE, head_count, head_width),
    )
    groups = [attend_tiles(queries, local_keys, local_values, permitted(0), scaling), text_group]
    extended = extended_2(image_pairs, (("rows", 1),), TILE)
    extended = extended.reshape(2, tiles_dev + 2, TILE, head_count, head_width)
    for offset in (-1, 1):
        groups.append(
            attend_tiles(
                queries,
                extended[0, 1 + offset : 1 + offset + tiles_dev],
                extended[1, 1 + offset : 1 + offset + tiles_dev],
                permitted(offset),
                scaling,
            )
        )
    gate_rows = lax.dynamic_index_in_dim(gate_table, timestep[0], 0, keepdims=False)
    attended = combine_groups(groups).reshape(rows_dev, width)
    image_out = (attended * gate_rows[0]).astype(jnp.bfloat16)
    text_flat = text_queries.reshape(-1, head_count, head_width)
    image_keys = image_pairs[0].reshape(rows_dev, head_count, head_width)
    image_values = image_pairs[1].reshape(rows_dev, head_count, head_width)
    every_key = jnp.ones((1, 1, rows_dev), dtype=bool)
    maxima, totals, summed = attend_rows(text_flat, image_keys, image_values, every_key, scaling)
    text_dev = text_query.shape[0]
    text_start = position * text_dev
    global_max = lax.pmax(maxima, "rows")
    factor = jnp.exp(maxima - global_max)
    scaled_summed = summed.astype(jnp.float32) * factor[..., None]
    scaled_totals = totals * factor
    whole_summed, whole_totals = lax.psum((scaled_summed, scaled_totals), "rows")
    shared_summed = lax.dynamic_slice_in_dim(whole_summed, text_start, text_dev, 0)
    shared_totals = lax.dynamic_slice_in_dim(whole_totals, text_start, text_dev, 0)
    remote = (
        lax.dynamic_slice_in_dim(global_max, text_start, text_dev, 0),
        shared_totals,
        shared_summed,
    )
    own_rows = text_query.reshape(text_dev, head_count, head_width)
    own_text = attend_rows(own_rows, text_keys, text_values, text_allowed, scaling)
    text_attended = combine_groups([remote, own_text]).reshape(text_dev, width)
    text_out = (text_attended * gate_rows[1]).astype(jnp.bfloat16)
    return (image_out, text_out)


def solution(mesh):
    placed = (
        P(("groups", "rows"), None),
        P(None, ("groups", "rows"), None),
        P(("groups", "rows"), None),
        P(None, ("groups", "rows"), None),
        P("groups"),
        P(),
        P(),
        P(),
    )
    return jax.shard_map(
        on_device,
        mesh=mesh,
        in_specs=placed,
        out_specs=(P(("groups", "rows"), None), P(("groups", "rows"), None)),
        check_vma=False,
    )
```

profile of v0, /device:TPU:0, one launch (start us, length us, event | category | flops | bytes accessed | tf_op | source)
XLA Modules:
  0.0 297.9 jit_solution(4161448792035331032)
XLA Ops:
  8.0 4.0 %collective-permute-start = (bf16[2,384,2048]{2,1,0:T(8,128)(2,1)}, bf16[2,384,2048]{2,1,0:T(8,128)(2,1)}, u32[]{:S(2)}, u32[]{:S(2)}) collective-permute-start(bf16[2,384,2048]{2,1,0:T(8,128)(2,1)} %param.9), channel_id=1, source_target_pairs={{0,1},{1,2},{2,3},{3,4},{4,5},{5,6},{6,7},{7,8},{8,9},{9,10},{10,1... | collective-permute-start | bytes 9437192 | tf_op jit(solution)/shard_map/ppermute | solution.py:19
  17.3 4.1 %fusion.134 = (bf16[1,384,2048]{2,1,0:T(8,128)(2,1)}, bf16[1,384,2048]{2,1,0:T(8,128)(2,1)}) fusion(bf16[2,384,2048]{2,1,0:T(8,128)(2,1)} %param.9), kind=kLoop, calls=%fused_computation.155 | loop fusion | bytes 6291456 | tf_op jit(solution)/shard_map/slice | solution.py:104
  28.3 3.6 %copy-done.2 = f32[16,384,384]{2,1,0:T(8,128)} copy-done((f32[16,384,384]{2,1,0:T(8,128)}, f32[16,384,384]{2,1,0:T(8,128)S(1)}, u32[]{:S(2)}) %copy-start.2) | copy-done | bytes 9437208
  31.9 3.5 %fusion.67 = bf16[16,384,128]{1,2,0:T(8,128)(2,1)} fusion(bf16[384,16,128]{0,2,1:T(8,128)(2,1)S(1)} %bitcast.291, f32[16,384,384]{2,1,0:T(8,128)S(1)} %get-tuple-element.26, f32[384,16]{0,1:T(8,128)S(1)} %get-tuple-element.25, pred[16]{0:T(512)(128)(4,1)S(1)} %get-tuple-element.24), kind=kOutput, calls=%fused_computation.81 | convolution fusion | flops 616562688 | bytes 12607504 | tf_op jit(solution)/shard_map/tqhk,tkhe->tqhe/dot_general | solution.py:37
  35.5 28.8 %all-gather.5.cloned.1.call-done = bf16[256,2048]{1,0:T(8,128)(2,1)} async-done(((bf16[16,2048]{1,0:T(8,128)(2,1)}), bf16[256,2048]{1,0:T(8,128)(2,1)}) %all-gather.5.cloned.1.call-update) | async-done | bytes 1048592 | tf_op jit(solution)/shard_map/all_gather | solution.py:97
  66.7 4.9 %bitcast_reduce_fusion.3 = (f32[256,16]{0,1:T(8,128)S(1)}, f32[16,384,256]{2,1,0:T(8,128)}) fusion(bf16[384,16,128]{0,2,1:T(8,128)(2,1)S(1)} %bitcast.287, bf16[256,16,128]{0,2,1:T(8,128)(2,1)} %bitcast.294), kind=kOutput, calls=%fused_computation.23 | convolution fusion | flops 405794816 | bytes 8929280 | tf_op jit(solution)/shard_map/qhe,khe->qhk/dot_general | solution.py:48
  71.6 66.7 %pmax.7 = f32[256,16]{0,1:T(8,128)S(1)} all-reduce(f32[256,16]{0,1:T(8,128)S(1)} %get-tuple-element.35), channel_id=1, replica_groups=mesh['groups'=2,'rows'=16] {'rows'}, use_global_device_ids=true, to_apply=%region_9.10 | all-reduce | flops 4096 | bytes 32768 | tf_op jit(solution)/shard_map/pmax | solution.py:143
  138.3 4.0 %fusion.15 = f32[256,16]{0,1:T(8,128)S(1)} fusion(f32[16,384,256]{2,1,0:T(8,128)} %get-tuple-element.36, f32[256,16]{0,1:T(8,128)S(1)} %get-tuple-element.35), kind=kLoop, calls=%fused_computation.30 | loop fusion | flops 4714496 | bytes 6324224 | tf_op jit(solution)/shard_map/reduce_sum | solution.py:53
  142.9 4.4 %bitcast_multiply_fusion.2 = f32[256,16,128]{2,0,1:T(8,128)} fusion(bf16[384,16,128]{0,2,1:T(8,128)(2,1)} %bitcast.290, f32[16,384,256]{2,1,0:T(8,128)S(1)} %copy-done.1, f32[256,16]{0,1:T(8,128)S(1)} %get-tuple-element.35, f32[256,16]{0,1:T(8,128)S(1)} %get-tuple-element.6), kind=kOutput, calls=%fused_computation.79 | convolution fusion | flops 408944640 | bytes 9994240 | tf_op jit(solution)/shard_map/qhk,khe->qhe/dot_general | solution.py:54
  147.3 58.2 %psum.15 = f32[256,16]{0,1:T(8,128)S(1)} all-reduce(f32[256,16]{0,1:T(8,128)S(1)} %get-tuple-element.5), channel_id=1, replica_groups=mesh['groups'=2,'rows'=16] {'rows'}, use_global_device_ids=true, to_apply=%region_13.14 | all-reduce | flops 4096 | bytes 32768 | tf_op jit(solution)/shard_map/psum | solution.py:147
  205.5 7.6 %pad_maximum_fusion = bf16[2,1152,2048]{2,1,0:T(8,128)(2,1)} fusion(bf16[2,384,2048]{2,1,0:T(8,128)(2,1)} %collective-permute-done.1, bf16[2,384,2048]{2,1,0:T(8,128)(2,1)} %param.9, bf16[2,384,2048]{2,1,0:T(8,128)(2,1)} %collective-permute-done), kind=kLoop, calls=%fused_computation | loop fusion | flops 28311552 | bytes 18874368 | tf_op jit(solution)/shard_map/concatenate | solution.py:17
  213.1 11.0 %copy.104 = bf16[288,8,16,128]{3,2,1,0:T(8,128)(2,1)} copy(bf16[288,8,16,128]{3,1,2,0:T(8,128)(2,1)} %bitcast.284) | data formatting | bytes 18874368
  224.2 5.6 %fusion.133 = (bf16[1,1,384,16,128]{4,3,2,1,0:T(8,128)(2,1)}, bf16[1,1,384,16,128]{4,3,2,1,0:T(8,128)(2,1)}, bf16[1,1,384,16,128]{4,3,2,1,0:T(8,128)(2,1)}, bf16[1,1,384,16,128]{4,3,2,1,0:T(8,128)(2,1)S(1)}) fusion(bf16[2,3,384,16,128]{4,3,2,1,0:T(8,128)(2,1)} %bitcast.285), kind=kLoop, calls=%fused_computation.154 | loop fusion | bytes 12582912 | tf_op jit(solution)/shard_map/slice | solution.py:128
  229.8 2.8 copy.99
  234.6 3.3 %bitcast_reduce_fusion = (f32[384,16]{0,1:T(8,128)S(1)}, f32[16,384,384]{2,1,0:T(8,128)S(1)}) fusion(pred[16]{0:T(512)(128)(4,1)S(1)} %get-tuple-element.23, bf16[1,1,384,16,128]{4,3,2,1,0:T(8,128)(2,1)} %get-tuple-element.13, bf16[384,2048]{1,0:T(8,128)(2,1)S(1)} %copy-done), kind=kOutput, calls=%fused_computation.2 | convolution fusion | flops 611051520 | bytes 12607504 | tf_op jit(solution)/shard_map/tqhe,tkhe->tqhk/dot_general | solution.py:30
  240.6 3.5 %fusion.73 = bf16[16,128,384]{2,1,0:T(8,128)(2,1)} fusion(f32[16,384,384]{2,1,0:T(8,128)S(1)} %get-tuple-element.28, f32[384,16]{0,1:T(8,128)S(1)} %get-tuple-element.27, pred[16]{0:T(512)(128)(4,1)S(1)} %get-tuple-element.23, bf16[1,1,384,16,128]{2,4,3,1,0:T(8,128)(2,1)S(1)} %copy-done.7), kind=kOutput, calls=%fused_computation.83 | convolution fusion | flops 616562688 | bytes 12607504 | tf_op jit(solution)/shard_map/tqhk,tkhe->tqhe/dot_general | solution.py:37
  246.3 5.5 %fusion.6 = (f32[384,16]{0,1:T(8,128)S(1)}, f32[384,16]{0,1:T(8,128)S(1)}) fusion(f32[16,384,384]{2,1,0:T(8,128)S(1)} %bitcast.283, f32[384,16]{0,1:T(8,128)S(1)} %get-tuple-element.25, pred[16]{0:T(512)(128)(4,1)S(1)} %get-tuple-element.24, f32[384,16]{0,1:T(8,128)S(1)} %get-tuple-element.29, f32[16,384,384]{2,1,0:T(8,128)S(1)} %get-tuple-element.30, ...), kind=kLoop, calls=%fused_computation.16 | loop fusion | flops 23580672 | bytes 18972704 | tf_op jit(solution)/shard_map/reduce_sum | solution.py:36
  251.8 3.5 %fusion.70 = bf16[16,128,384]{2,1,0:T(8,128)(2,1)} fusion(f32[16,384,384]{2,1,0:T(8,128)S(1)} %get-tuple-element.30, f32[384,16]{0,1:T(8,128)S(1)} %get-tuple-element.29, pred[16]{0:T(512)(128)(4,1)S(1)} %get-tuple-element.22, bf16[1,1,384,16,128]{2,4,3,1,0:T(8,128)(2,1)S(1)} %copy-done.6), kind=kOutput, calls=%fused_computation.82 | convolution fusion | flops 616562688 | bytes 12607504 | tf_op jit(solution)/shard_map/tqhk,tkhe->tqhe/dot_general | solution.py:37
  255.4 6.8 %fusion.135 = (bf16[1,256,2048]{2,0,1:T(2,128)(2,1)}, bf16[1,256,2048]{2,0,1:T(2,128)(2,1)}) fusion(bf16[2,256,2048]{2,0,1:T(2,128)(2,1)} %all-gather.3.cloned.1.call-done), kind=kLoop, calls=%fused_computation.156 | loop fusion | bytes 4194304 | tf_op jit(solution)/shard_map/slice | solution.py:101
  262.2 5.8 %copy.67 = bf16[1,256,2048]{1,2,0:T(8,128)(2,1)} copy(bf16[1,256,2048]{2,0,1:T(2,128)(2,1)} %get-tuple-element.18) | data formatting | bytes 2097152 | tf_op jit(solution)/shard_map/slice | solution.py:101
  268.0 4.8 %copy.96 = bf16[1,256,2048]{1,2,0:T(8,128)(2,1)S(1)} copy(bf16[1,256,2048]{2,0,1:T(2,128)(2,1)} %get-tuple-element.19) | data formatting | bytes 2097152
  276.9 4.5 %fusion.52 = f32[1,384,16,128]{1,3,2,0:T(8,128)} fusion(bf16[16,384,128]{1,2,0:T(8,128)(2,1)S(1)} %copy-done.10, bf16[16,128,384]{2,1,0:T(8,128)(2,1)S(1)} %copy-done.11, bf16[16,128,384]{2,1,0:T(8,128)(2,1)S(1)} %copy-done.12, f32[384,16]{0,1:T(8,128)S(1)} %get-tuple-element.7, f32[384,16]{0,1:T(8,128)S(1)} %get-tuple-element.11, ...), kind=kOutput, calls=%fused_computation.63 | convolution fusion | flops 420741120 | bytes 15352064 | tf_op jit(solution)/shard_map/qhk,khe->qhe/dot_general | solution.py:54
  281.4 3.6 %copy.73 = f32[384,2048]{1,0:T(8,128)} copy(f32[384,2048]{0,1:T(8,128)} %bitcast.295) | data formatting | bytes 6291456 | tf_op jit(solution)/shard_map/reshape | solution.py:134
  288.0 3.4 %multiply_convert_fusion = bf16[384,2048]{1,0:T(8,128)(2,1)} fusion(f32[384,2048]{1,0:T(8,128)} %copy.73, f32[2048]{0:T(1024)S(1)} %bitcast.296), kind=kLoop, calls=%fused_computation.72 | loop fusion | flops 1572864 | bytes 4726784 | tf_op jit(solution)/shard_map/convert_element_type | solution.py:135
  (63 shorter events, 29.2 us)
Async XLA Ops:
  7.2 18.7 %copy-start = (bf16[384,2048]{1,0:T(8,128)(2,1)S(1)}, bf16[384,2048]{1,0:T(8,128)(2,1)}, u32[]{:S(2)}) copy-start(bf16[384,2048]{1,0:T(8,128)(2,1)} %param.8) | copy-start | bytes 4718596
  7.2 57.1 %all-gather.5.cloned.1.call-start = ((), (), s32[]{:S(2)}) async-start(), calls=%async_computation.1 | async-start | bytes 1114112 | tf_op jit(solution)/shard_map/all_gather | solution.py:97
  7.9 247.5 %all-gather.3.cloned.1.call-start = ((), (), s32[]{:S(2)}) async-start(), calls=%async_computation | async-start | bytes 2228224 | tf_op jit(solution)/shard_map/all_gather | solution.py:98
  8.0 197.5 %collective-permute-start = (bf16[2,384,2048]{2,1,0:T(8,128)(2,1)}, bf16[2,384,2048]{2,1,0:T(8,128)(2,1)}, u32[]{:S(2)}, u32[]{:S(2)}) collective-permute-start(bf16[2,384,2048]{2,1,0:T(8,128)(2,1)} %param.9), channel_id=1, source_target_pairs={{0,1},{1,2},{2,3},{3,4},{4,5},{5,6},{6,7},{7,8},{8,9},{9,10},{10,1... | collective-permute-start | bytes 9437192 | tf_op jit(solution)/shard_map/ppermute | solution.py:19
  12.0 193.5 %collective-permute-start.1 = (bf16[2,384,2048]{2,1,0:T(8,128)(2,1)}, bf16[2,384,2048]{2,1,0:T(8,128)(2,1)}, u32[]{:S(2)}, u32[]{:S(2)}) collective-permute-start(bf16[2,384,2048]{2,1,0:T(8,128)(2,1)} %param.9), channel_id=1, source_target_pairs={{1,0},{2,1},{3,2},{4,3},{5,4},{6,5},{7,6},{8,7},{9,8},{10,9},{11,1... | collective-permute-start | bytes 9437192 | tf_op jit(solution)/shard_map/ppermute | solution.py:21
  15.0 270.7 %all-reduce.2.cloned.1.call-start = ((), (), s32[]{:S(2)}) async-start(), calls=%async_computation.2 | async-start | bytes 4194304 | tf_op jit(solution)/shard_map/psum | solution.py:147
  17.3 4.1 %copy-start.9 = (s32[256]{0:T(256)S(1)}, s32[256]{0:T(256)}, u32[]{:S(2)}) copy-start(s32[256]{0:T(256)} %param.12) | copy-start | bytes 3076
  25.8 6.1 %copy-start.3 = (bf16[1,384,2048]{1,2,0:T(8,128)(2,1)S(1)}, bf16[1,384,2048]{1,2,0:T(8,128)(2,1)}, u32[]{:S(2)}) copy-start(bf16[1,384,2048]{1,2,0:T(8,128)(2,1)} %copy.57) | copy-start | bytes 4718596
  28.3 3.6 %copy-start.2 = (f32[16,384,384]{2,1,0:T(8,128)}, f32[16,384,384]{2,1,0:T(8,128)S(1)}, u32[]{:S(2)}) copy-start(f32[16,384,384]{2,1,0:T(8,128)S(1)} %get-tuple-element.26) | copy-start | bytes 28311556
  138.3 4.6 %copy-start.1 = (f32[16,384,256]{2,1,0:T(8,128)S(1)}, f32[16,384,256]{2,1,0:T(8,128)}, u32[]{:S(2)}) copy-start(f32[16,384,256]{2,1,0:T(8,128)} %get-tuple-element.36) | copy-start | bytes 18874372
  237.9 2.7 copy-start.7
  240.6 3.5 %copy-start.5 = (bf16[1,1,384,16,128]{4,3,2,1,0:T(8,128)(2,1)S(1)}, bf16[1,1,384,16,128]{4,3,2,1,0:T(8,128)(2,1)}, u32[]{:S(2)}) copy-start(bf16[1,1,384,16,128]{4,3,2,1,0:T(8,128)(2,1)} %get-tuple-element.14) | copy-start | bytes 4718596
  240.6 5.4 %slice-start = ((s8[9437184]{0:T(1024)(128)(4,1)}), s8[4194304]{0:T(1024)(128)(4,1)S(1)}, s32[]{:S(2)}) async-start(s8[9437184]{0:T(1024)(128)(4,1)} %bitcast.282), calls=%async_computation.3 | async-start | bytes 8388608
  240.6 5.4 %slice-start.1 = ((s8[9437184]{0:T(1024)(128)(4,1)}), s8[1048576]{0:T(1024)(128)(4,1)S(1)}, s32[]{:S(2)}) async-start(s8[9437184]{0:T(1024)(128)(4,1)} %bitcast.282), calls=%async_computation.4 | async-start | bytes 2097152
  244.1 2.2 slice-start.2
  246.3 5.5 %copy-start.6 = (bf16[1,1,384,16,128]{2,4,3,1,0:T(8,128)(2,1)S(1)}, bf16[1,1,384,16,128]{2,4,3,1,0:T(8,128)(2,1)}, u32[]{:S(2)}) copy-start(bf16[1,1,384,16,128]{2,4,3,1,0:T(8,128)(2,1)} %copy.99) | copy-start | bytes 4718596
  274.2 1.8 copy-start.4
  274.2 1.8 copy-start.10
  274.2 2.2 copy-start.11
  274.2 2.7 copy-start.12
  281.4 3.6 %copy-start.8 = (bf16[16,2048]{1,0:T(8,128)(2,1)S(1)}, bf16[16,2048]{1,0:T(8,128)(2,1)}, u32[]{:S(2)}) copy-start(bf16[16,2048]{1,0:T(8,128)(2,1)} %param.10) | copy-start | bytes 196612
Sparse Core Ops, SparseCore 0:
  10.2 54.0 all-gather.4
  66.5 43.8 all-gather.2
  147.5 95.1 all-reduce.1
where the time goes:
time: 299 us; the launch traced here: 298 us
  blocking collectives  125 us (42%)
  local copies, waits for them, and re-layouts  61.2 us (20%)
  matrix products  35.5 us (12%)
  waiting for transfers between devices  29.6 us (10%)
  other arithmetic  26.6 us (9%)
  between operations  14.7 us (5%)
  starting transfers between devices  5.42 us (2%)
    pmax x1, blocking collectives, on_device(): global_max = lax.pmax(maxima, 'rows')  66.7 us
    psum x1, blocking collectives, on_device(): lax.psum((scaled_summed, scaled_totals), 'rows')  58.2 us
    unnamed x38, local copies, waits for them, and re-layouts  29.6 us
    all_gather x1, waiting for transfers between devices, on_device(): lax.all_gather(text_query, 'rows', axis=0, tiled=True)  28.8 us
    slice x2, local copies, waits for them, and re-layouts, on_device(): text_values = text_gathered[1].reshape(-1, head_count, head_width)  12.6 us
    dot_general x3, matrix products, attend_tiles(): jnp.einsum('tqhk,tkhe->tqhe', exponent.astype(jnp.bfloat16), value_rows,...  10.6 us
    dot_general x3, matrix products, attend_rows(): jnp.einsum('qhk,khe->qhe', exponent.astype(jnp.bfloat16), value_rows, pre...  10.5 us
    reduce_sum x2, other arithmetic, attend_tiles(): totals = jnp.sum(exponent, axis=-1)  8.14 us
  transfers between devices with their start and end apart: 5, of which 1 were waited for; matrix products, arithmetic and copies ran while one was open for 38% of the time, Pallas kernels for 0%

commit v1 on v0

--- a/solution.py
+++ b/solution.py
@@ -6,6 +6,18 @@
 
 TILE = 384
 masked_score = -1e30
+
+
+def gather_by_bits(x, axis, dim):
+    ways, here = (lax.axis_size(axis), lax.axis_index(axis))
+    grown, reach = (x, 1)
+    while reach < ways:
+        theirs = lax.ppermute(grown, axis, [(d, d ^ reach) for d in range(ways)])
+        mine_first = jnp.concatenate([grown, theirs], axis=dim)
+        theirs_first = jnp.concatenate([theirs, grown], axis=dim)
+        grown = jnp.where(here & reach == 0, mine_first, theirs_first)
+        reach = 2 * reach
+    return grown
 
 
 def extended_2(cells, sides, width):
@@ -94,7 +106,7 @@
     reach_back = window_offsets[:, 0]
     reach_ahead = window_offsets[:, 1]
     text_queries, text_gathered = (
-        lax.all_gather(text_query, "rows", axis=0, tiled=True),
+        gather_by_bits(text_query, "rows", 0),
         lax.all_gather(text_pairs, "rows", axis=1, tiled=True),
     )
     text_keys = text_gathered[0].reshape(-1, head_count, head_width)

time: 299 us -> 348 us (1.16)
  starting transfers between devices: 5.42 us -> 44.7 us
  waiting for transfers between devices: 29.6 us -> 50.8 us
  blocking collectives: 125 us -> 119 us
  local copies, waits for them, and re-layouts: 61.2 us -> 56.4 us
    ppermute x0 -> x4, waiting for transfers between devices: none -> 50.7 us  [gather_by_bits(): theirs = lax.ppermute(grown, axis, [(d, d ^ reach) for d in range(ways)])]
    ppermute x0 -> x4, starting transfers between devices: none -> 39.1 us  [gather_by_bits(): theirs = lax.ppermute(grown, axis, [(d, d ^ reach) for d in range(ways)])]
    all_gather x1 -> x0, waiting for transfers between devices: 28.8 us -> none  [on_device(): lax.all_gather(text_query, 'rows', axis=0, tiled=True)]
    pmax x1, blocking collectives: 66.7 us -> 60.9 us  [on_device(): global_max = lax.pmax(maxima, 'rows')]
    unnamed x38 -> x40, local copies, waits for them, and re-layouts: 29.6 us -> 26 us
  transfers between devices with their start and end apart: 5 -> 8, of which waited for: 1 -> 3; matrix products, arithmetic and copies ran while one was open for 38% -> 32% of each run, Pallas kernels for 0% -> 0%
where the time goes in v1:
time: 348 us; the launch traced here: 347 us
  blocking collectives  119 us (34%)
  local copies, waits for them, and re-layouts  56.4 us (16%)
  waiting for transfers between devices  50.8 us (15%)
  starting transfers between devices  44.7 us (13%)
  matrix products  34.3 us (10%)
  other arithmetic  26.3 us (8%)
  between operations  15.1 us (4%)
    pmax x1, blocking collectives, on_device(): global_max = lax.pmax(maxima, 'rows')  60.9 us
    psum x1, blocking collectives, on_device(): lax.psum((scaled_summed, scaled_totals), 'rows')  58.2 us
    ppermute x4, waiting for transfers between devices, gather_by_bits(): theirs = lax.ppermute(grown, axis, [(d, d ^ reach) for d in range(ways)])  50.7 us
    ppermute x4, starting transfers between devices, gather_by_bits(): theirs = lax.ppermute(grown, axis, [(d, d ^ reach) for d in range(ways)])  39.1 us
    unnamed x40, local copies, waits for them, and re-layouts  26 us
    slice x2, local copies, waits for them, and re-layouts, on_device(): text_values = text_gathered[1].reshape(-1, head_count, head_width)  12.7 us
    dot_general x3, matrix products, attend_tiles(): jnp.einsum('tqhk,tkhe->tqhe', exponent.astype(jnp.bfloat16), value_rows,...  11.2 us
    dot_general x3, matrix products, attend_rows(): jnp.einsum('qhk,khe->qhe', exponent.astype(jnp.bfloat16), value_rows, pre...  10 us
  transfers between devices with their start and end apart: 8, of which 3 were waited for; matrix products, arithmetic and copies ran while one was open for 32% of the time, Pallas kernels for 0%

profile of v1, /device:TPU:0, one launch (start us, length us, event | category | flops | bytes accessed | tf_op | source)
XLA Modules:
  0.0 346.7 jit_solution(11941241099091726124)
XLA Ops:
  7.2 4.2 %collective-permute-start = (bf16[2,384,2048]{2,1,0:T(8,128)(2,1)}, bf16[2,384,2048]{2,1,0:T(8,128)(2,1)}, u32[]{:S(2)}, u32[]{:S(2)}) collective-permute-start(bf16[2,384,2048]{2,1,0:T(8,128)(2,1)} %param.9), channel_id=1, source_target_pairs={{0,1},{1,2},{2,3},{3,4},{4,5},{5,6},{6,7},{7,8},{8,9},{9,10},{10,1... | collective-permute-start | bytes 9437192 | tf_op jit(solution)/shard_map/ppermute | solution.py:31
  17.0 4.1 %fusion.140 = (bf16[1,384,2048]{2,1,0:T(8,128)(2,1)}, bf16[1,384,2048]{2,1,0:T(8,128)(2,1)}) fusion(bf16[2,384,2048]{2,1,0:T(8,128)(2,1)} %param.9), kind=kLoop, calls=%fused_computation.173 | loop fusion | bytes 6291456 | tf_op jit(solution)/shard_map/slice | solution.py:116
  28.8 4.1 %fusion.67 = bf16[16,384,128]{1,2,0:T(8,128)(2,1)} fusion(bf16[384,16,128]{0,2,1:T(8,128)(2,1)S(1)} %bitcast.311, f32[16,384,384]{2,1,0:T(8,128)S(1)} %get-tuple-element.26, f32[384,16]{0,1:T(8,128)S(1)} %get-tuple-element.25, pred[16]{0:T(512)(128)(4,1)S(1)} %get-tuple-element.24), kind=kOutput, calls=%fused_computation.81 | convolution fusion | flops 616562688 | bytes 12607504 | tf_op jit(solution)/shard_map/tqhk,tkhe->tqhe/dot_general | solution.py:49
  35.5 25.7 %collective-permute-done.3 = bf16[32,2048]{1,0:T(8,128)(2,1)S(1)} collective-permute-done((bf16[32,2048]{1,0:T(8,128)(2,1)S(1)}, bf16[32,2048]{1,0:T(8,128)(2,1)S(1)}, u32[]{:S(2)}, u32[]{:S(2)}) %collective-permute-start.3) | collective-permute-done | bytes 131104 | tf_op jit(solution)/shard_map/ppermute | solution.py:15
  61.2 32.5 %collective-permute-start.4 = (bf16[64,2048]{1,0:T(8,128)(2,1)S(1)}, bf16[64,2048]{1,0:T(8,128)(2,1)S(1)}, u32[]{:S(2)}, u32[]{:S(2)}) collective-permute-start(bf16[64,2048]{1,0:T(8,128)(2,1)S(1)} %maximum_select_fusion.5), channel_id=1, source_target_pairs={{0,4},{1,5},{2,6},{3,7},{4,0},{5,1},{6,2},{7,3},{8,12},{9,13},{10,... | collective-permute-start | bytes 786440 | tf_op jit(solution)/shard_map/ppermute | solution.py:15
  93.8 4.8 %collective-permute-done.4 = bf16[64,2048]{1,0:T(8,128)(2,1)S(1)} collective-permute-done((bf16[64,2048]{1,0:T(8,128)(2,1)S(1)}, bf16[64,2048]{1,0:T(8,128)(2,1)S(1)}, u32[]{:S(2)}, u32[]{:S(2)}) %collective-permute-start.4) | collective-permute-done | bytes 262176 | tf_op jit(solution)/shard_map/ppermute | solution.py:15
  102.3 20.2 %collective-permute-done.5 = bf16[128,2048]{1,0:T(8,128)(2,1)S(1)} collective-permute-done((bf16[128,2048]{1,0:T(8,128)(2,1)S(1)}, bf16[128,2048]{1,0:T(8,128)(2,1)S(1)}, u32[]{:S(2)}, u32[]{:S(2)}) %collective-permute-start.5) | collective-permute-done | bytes 524320 | tf_op jit(solution)/shard_map/ppermute | solution.py:15
  122.7 3.7 %bitcast_reduce_fusion.3 = (f32[256,16]{0,1:T(8,128)S(1)}, f32[16,256,384]{2,1,0:T(8,128)}) fusion(bf16[384,16,128]{0,2,1:T(8,128)(2,1)S(1)} %bitcast.307, bf16[128,16,128]{2,0,1:T(8,128)(2,1)S(1)} %copy_bitcast_fusion.4, bf16[128,16,128]{2,0,1:T(8,128)(2,1)S(1)} %maximum_select_fusion.2, pred[]{:T(512)S(6)} %eq.20), kind=kOutput, calls=%fused_computation.23 | convolution fusion | flops 410513408 | bytes 8929281 | tf_op jit(solution)/shard_map/qhe,khe->qhk/dot_general | solution.py:60
  126.3 60.9 %pmax.7 = f32[256,16]{0,1:T(8,128)S(1)} all-reduce(f32[256,16]{0,1:T(8,128)S(1)} %get-tuple-element.35), channel_id=1, replica_groups=mesh['groups'=2,'rows'=16] {'rows'}, use_global_device_ids=true, to_apply=%region_9.10 | all-reduce | flops 4096 | bytes 32768 | tf_op jit(solution)/shard_map/pmax | solution.py:155
  187.3 4.0 %fusion.15 = f32[256,16]{0,1:T(8,128)S(1)} fusion(f32[16,256,384]{2,1,0:T(8,128)} %get-tuple-element.36, f32[256,16]{0,1:T(8,128)S(1)} %get-tuple-element.35), kind=kLoop, calls=%fused_computation.30 | loop fusion | flops 4714496 | bytes 6324224 | tf_op jit(solution)/shard_map/reduce_sum | solution.py:65
  191.9 3.9 %bitcast_multiply_fusion.2 = f32[256,16,128]{2,0,1:T(8,128)} fusion(bf16[384,16,128]{0,2,1:T(8,128)(2,1)} %bitcast.310, f32[16,256,384]{2,1,0:T(8,128)S(1)} %copy-done.1, f32[256,16]{0,1:T(8,128)S(1)} %get-tuple-element.35, f32[256,16]{0,1:T(8,128)S(1)} %get-tuple-element.6), kind=kOutput, calls=%fused_computation.79 | convolution fusion | flops 408944640 | bytes 9994240 | tf_op jit(solution)/shard_map/qhk,khe->qhe/dot_general | solution.py:66
  195.8 58.2 %psum.15 = f32[256,16]{0,1:T(8,128)S(1)} all-reduce(f32[256,16]{0,1:T(8,128)S(1)} %get-tuple-element.5), channel_id=1, replica_groups=mesh['groups'=2,'rows'=16] {'rows'}, use_global_device_ids=true, to_apply=%region_13.14 | all-reduce | flops 4096 | bytes 32768 | tf_op jit(solution)/shard_map/psum | solution.py:159
  254.1 7.6 %pad_maximum_fusion = bf16[2,1152,2048]{2,1,0:T(8,128)(2,1)} fusion(bf16[2,384,2048]{2,1,0:T(8,128)(2,1)} %collective-permute-done.1, bf16[2,384,2048]{2,1,0:T(8,128)(2,1)} %param.9, bf16[2,384,2048]{2,1,0:T(8,128)(2,1)} %collective-permute-done), kind=kLoop, calls=%fused_computation | loop fusion | flops 28311552 | bytes 18874368 | tf_op jit(solution)/shard_map/concatenate | solution.py:29
  261.7 11.0 %copy.129 = bf16[288,8,16,128]{3,2,1,0:T(8,128)(2,1)} copy(bf16[288,8,16,128]{3,1,2,0:T(8,128)(2,1)} %bitcast.304) | data formatting | bytes 18874368
  272.7 5.6 %fusion.139 = (bf16[1,1,384,16,128]{4,3,2,1,0:T(8,128)(2,1)}, bf16[1,1,384,16,128]{4,3,2,1,0:T(8,128)(2,1)}, bf16[1,1,384,16,128]{4,3,2,1,0:T(8,128)(2,1)}, bf16[1,1,384,16,128]{4,3,2,1,0:T(8,128)(2,1)S(1)}) fusion(bf16[2,3,384,16,128]{4,3,2,1,0:T(8,128)(2,1)} %bitcast.305), kind=kLoop, calls=%fused_computation.172 | loop fusion | bytes 12582912 | tf_op jit(solution)/shard_map/slice | solution.py:140
  289.2 3.5 %fusion.73 = bf16[16,128,384]{2,1,0:T(8,128)(2,1)} fusion(f32[16,384,384]{2,1,0:T(8,128)S(1)} %get-tuple-element.28, f32[384,16]{0,1:T(8,128)S(1)} %get-tuple-element.27, pred[16]{0:T(512)(128)(4,1)S(1)} %get-tuple-element.23, bf16[1,1,384,16,128]{2,4,3,1,0:T(8,128)(2,1)S(1)} %copy-done.7), kind=kOutput, calls=%fused_computation.83 | convolution fusion | flops 616562688 | bytes 12607504 | tf_op jit(solution)/shard_map/tqhk,tkhe->tqhe/dot_general | solution.py:49
  294.9 5.5 %fusion.6 = (f32[384,16]{0,1:T(8,128)S(1)}, f32[384,16]{0,1:T(8,128)S(1)}) fusion(f32[16,384,384]{2,1,0:T(8,128)S(1)} %bitcast.303, f32[384,16]{0,1:T(8,128)S(1)} %get-tuple-element.25, pred[16]{0:T(512)(128)(4,1)S(1)} %get-tuple-element.24, f32[384,16]{0,1:T(8,128)S(1)} %get-tuple-element.29, f32[16,384,384]{2,1,0:T(8,128)S(1)} %get-tuple-element.30, ...), kind=kLoop, calls=%fused_computation.16 | loop fusion | flops 23580672 | bytes 18972704 | tf_op jit(solution)/shard_map/reduce_sum | solution.py:48
  300.4 3.6 %fusion.70 = bf16[16,128,384]{2,1,0:T(8,128)(2,1)} fusion(f32[16,384,384]{2,1,0:T(8,128)S(1)} %get-tuple-element.30, f32[384,16]{0,1:T(8,128)S(1)} %get-tuple-element.29, pred[16]{0:T(512)(128)(4,1)S(1)} %get-tuple-element.22, bf16[1,1,384,16,128]{2,4,3,1,0:T(8,128)(2,1)S(1)} %copy-done.6), kind=kOutput, calls=%fused_computation.82 | convolution fusion | flops 616562688 | bytes 12607504 | tf_op jit(solution)/shard_map/tqhk,tkhe->tqhe/dot_general | solution.py:49
  303.9 6.9 %fusion.141 = (bf16[1,256,2048]{2,0,1:T(2,128)(2,1)}, bf16[1,256,2048]{2,0,1:T(2,128)(2,1)}) fusion(bf16[2,256,2048]{2,0,1:T(2,128)(2,1)} %all-gather.2.cloned.1.call-done), kind=kLoop, calls=%fused_computation.174 | loop fusion | bytes 4194304 | tf_op jit(solution)/shard_map/slice | solution.py:113
  310.8 5.8 %copy.83 = bf16[1,256,2048]{1,2,0:T(8,128)(2,1)} copy(bf16[1,256,2048]{2,0,1:T(2,128)(2,1)} %get-tuple-element.18) | data formatting | bytes 2097152 | tf_op jit(solution)/shard_map/slice | solution.py:113
  316.6 4.8 %copy.117 = bf16[1,256,2048]{1,2,0:T(8,128)(2,1)S(1)} copy(bf16[1,256,2048]{2,0,1:T(2,128)(2,1)} %get-tuple-element.19) | data formatting | bytes 2097152
  325.5 4.5 %fusion.52 = f32[1,384,16,128]{1,3,2,0:T(8,128)} fusion(bf16[16,384,128]{1,2,0:T(8,128)(2,1)S(1)} %copy-done.11, bf16[16,128,384]{2,1,0:T(8,128)(2,1)S(1)} %copy-done.12, bf16[16,128,384]{2,1,0:T(8,128)(2,1)S(1)} %copy-done.13, f32[384,16]{0,1:T(8,128)S(1)} %get-tuple-element.7, f32[384,16]{0,1:T(8,128)S(1)} %get-tuple-element.11, ...), kind=kOutput, calls=%fused_computation.63 | convolution fusion | flops 420741120 | bytes 15352064 | tf_op jit(solution)/shard_map/qhk,khe->qhe/dot_general | solution.py:66
  330.0 3.6 %copy.89 = f32[384,2048]{1,0:T(8,128)} copy(f32[384,2048]{0,1:T(8,128)} %bitcast.314) | data formatting | bytes 6291456 | tf_op jit(solution)/shard_map/reshape | solution.py:146
  336.5 3.4 multiply_convert_fusion
  (80 shorter events, 39.7 us)
Async XLA Ops:
  7.2 19.0 %copy-start = (bf16[384,2048]{1,0:T(8,128)(2,1)S(1)}, bf16[384,2048]{1,0:T(8,128)(2,1)}, u32[]{:S(2)}) copy-start(bf16[384,2048]{1,0:T(8,128)(2,1)} %param.8) | copy-start | bytes 4718596
  7.2 296.8 %all-gather.2.cloned.1.call-start = ((), (), s32[]{:S(2)}) async-start(), calls=%async_computation | async-start | bytes 2228224 | tf_op jit(solution)/shard_map/all_gather | solution.py:110
  7.2 246.8 %collective-permute-start = (bf16[2,384,2048]{2,1,0:T(8,128)(2,1)}, bf16[2,384,2048]{2,1,0:T(8,128)(2,1)}, u32[]{:S(2)}, u32[]{:S(2)}) collective-permute-start(bf16[2,384,2048]{2,1,0:T(8,128)(2,1)} %param.9), channel_id=1, source_target_pairs={{0,1},{1,2},{2,3},{3,4},{4,5},{5,6},{6,7},{7,8},{8,9},{9,10},{10,1... | collective-permute-start | bytes 9437192 | tf_op jit(solution)/shard_map/ppermute | solution.py:31
  11.4 242.7 %collective-permute-start.1 = (bf16[2,384,2048]{2,1,0:T(8,128)(2,1)}, bf16[2,384,2048]{2,1,0:T(8,128)(2,1)}, u32[]{:S(2)}, u32[]{:S(2)}) collective-permute-start(bf16[2,384,2048]{2,1,0:T(8,128)(2,1)} %param.9), channel_id=1, source_target_pairs={{1,0},{2,1},{3,2},{4,3},{5,4},{6,5},{7,6},{8,7},{9,8},{10,9},{11,1... | collective-permute-start | bytes 9437192 | tf_op jit(solution)/shard_map/ppermute | solution.py:33
  12.7 21.0 %collective-permute-start.2 = (bf16[16,2048]{1,0:T(8,128)(2,1)}, bf16[16,2048]{1,0:T(8,128)(2,1)S(1)}, u32[]{:S(2)}, u32[]{:S(2)}) collective-permute-start(bf16[16,2048]{1,0:T(8,128)(2,1)} %param.10), channel_id=1, source_target_pairs={{0,1},{1,0},{2,3},{3,2},{4,5},{5,4},{6,7},{7,6},{8,9},{9,8},{10,11... | collective-permute-start | bytes 196616 | tf_op jit(solution)/shard_map/ppermute | solution.py:15
  16.1 318.1 %all-reduce.2.cloned.1.call-start = ((), (), s32[]{:S(2)}) async-start(), calls=%async_computation.1 | async-start | bytes 4194304 | tf_op jit(solution)/shard_map/psum | solution.py:159
  21.7 4.5 %copy-start.9 = (s32[16,2]{0,1:T(2,128)S(1)}, s32[16,2]{0,1:T(2,128)}, u32[]{:S(2)}) copy-start(s32[16,2]{0,1:T(2,128)} %param.13) | copy-start | bytes 388
  26.2 2.5 copy-start.3
  28.7 4.2 %copy-start.2 = (f32[16,384,384]{2,1,0:T(8,128)}, f32[16,384,384]{2,1,0:T(8,128)S(1)}, u32[]{:S(2)}) copy-start(f32[16,384,384]{2,1,0:T(8,128)S(1)} %get-tuple-element.26) | copy-start | bytes 28311556
  28.7 5.0 %copy-start.8 = (bf16[16,2048]{1,0:T(8,128)(2,1)S(1)}, bf16[16,2048]{1,0:T(8,128)(2,1)}, u32[]{:S(2)}) copy-start(bf16[16,2048]{1,0:T(8,128)(2,1)} %param.10) | copy-start | bytes 196612
  28.7 6.7 %copy-start.10 = (s32[256]{0:T(256)S(1)}, s32[256]{0:T(256)}, u32[]{:S(2)}) copy-start(s32[256]{0:T(256)} %param.12) | copy-start | bytes 3076
  33.8 27.4 %collective-permute-start.3 = (bf16[32,2048]{1,0:T(8,128)(2,1)S(1)}, bf16[32,2048]{1,0:T(8,128)(2,1)S(1)}, u32[]{:S(2)}, u32[]{:S(2)}) collective-permute-start(bf16[32,2048]{1,0:T(8,128)(2,1)S(1)} %maximum_select_fusion.7), channel_id=1, source_target_pairs={{0,2},{1,3},{2,0},{3,1},{4,6},{5,7},{6,4},{7,5},{8,10},{9,11},{10,... | collective-permute-start | bytes 393224 | tf_op jit(solution)/shard_map/ppermute | solution.py:15
  61.2 37.4 %collective-permute-start.4 = (bf16[64,2048]{1,0:T(8,128)(2,1)S(1)}, bf16[64,2048]{1,0:T(8,128)(2,1)S(1)}, u32[]{:S(2)}, u32[]{:S(2)}) collective-permute-start(bf16[64,2048]{1,0:T(8,128)(2,1)S(1)} %maximum_select_fusion.5), channel_id=1, source_target_pairs={{0,4},{1,5},{2,6},{3,7},{4,0},{5,1},{6,2},{7,3},{8,12},{9,13},{10,... | collective-permute-start | bytes 786440 | tf_op jit(solution)/shard_map/ppermute | solution.py:15
  98.7 23.8 %collective-permute-start.5 = (bf16[128,2048]{1,0:T(8,128)(2,1)S(1)}, bf16[128,2048]{1,0:T(8,128)(2,1)S(1)}, u32[]{:S(2)}, u32[]{:S(2)}) collective-permute-start(bf16[128,2048]{1,0:T(8,128)(2,1)S(1)} %maximum_select_fusion.3), channel_id=1, source_target_pairs={{0,8},{1,9},{2,10},{3,11},{4,12},{5,13},{6,14},{7,15},{8,0},{9,1},... | collective-permute-start | bytes 1572872 | tf_op jit(solution)/shard_map/ppermute | solution.py:15
  187.3 4.6 %copy-start.1 = (f32[16,256,384]{2,1,0:T(8,128)S(1)}, f32[16,256,384]{2,1,0:T(8,128)}, u32[]{:S(2)}) copy-start(f32[16,256,384]{2,1,0:T(8,128)} %get-tuple-element.36) | copy-start | bytes 18874372
  286.5 2.7 copy-start.7
  289.2 3.5 %copy-start.5 = (bf16[1,1,384,16,128]{4,3,2,1,0:T(8,128)(2,1)S(1)}, bf16[1,1,384,16,128]{4,3,2,1,0:T(8,128)(2,1)}, u32[]{:S(2)}) copy-start(bf16[1,1,384,16,128]{4,3,2,1,0:T(8,128)(2,1)} %get-tuple-element.14) | copy-start | bytes 4718596
  289.2 5.4 %slice-start = ((s8[9437184]{0:T(1024)(128)(4,1)}), s8[4194304]{0:T(1024)(128)(4,1)S(1)}, s32[]{:S(2)}) async-start(s8[9437184]{0:T(1024)(128)(4,1)} %bitcast.302), calls=%async_computation.2 | async-start | bytes 8388608
  289.2 5.4 %slice-start.1 = ((s8[9437184]{0:T(1024)(128)(4,1)}), s8[1048576]{0:T(1024)(128)(4,1)S(1)}, s32[]{:S(2)}) async-start(s8[9437184]{0:T(1024)(128)(4,1)} %bitcast.302), calls=%async_computation.3 | async-start | bytes 2097152
  292.7 2.2 slice-start.2
  294.9 5.5 %copy-start.6 = (bf16[1,1,384,16,128]{2,4,3,1,0:T(8,128)(2,1)S(1)}, bf16[1,1,384,16,128]{2,4,3,1,0:T(8,128)(2,1)}, u32[]{:S(2)}) copy-start(bf16[1,1,384,16,128]{2,4,3,1,0:T(8,128)(2,1)} %copy.120) | copy-start | bytes 4718596
  322.8 1.8 copy-start.4
  322.8 2.2 copy-start.12
  322.8 2.7 copy-start.13
  (1 other events, 1.8 us)
Sparse Core Ops, SparseCore 0:
  16.2 53.8 all-gather.1
  195.9 95.2 all-reduce.1
